TPU v7x, 128 devices: a whole 4x4x4 slice. The times are simulated.
128 devices in a mesh: prefix: 16 (over z, y), group: 8 (over x, core).
Axes of the slice: x: 4, y: 4, z: 4, core: 2. Of those that a mesh axis runs over, the one named last changes fastest.
Arguments:
- queries: bfloat16 [16, 256, 8192], P(None, 'group', 'prefix'), may hold values from -128 to 128
- cand_kv: bfloat16 [16, 256, 2048], P(None, 'group'), may hold values from -32 to 32
- prefix_kv: bfloat16 [16384, 2048], P('prefix'), may hold values from -32 to 32
- lengths: int32 [16], replicated, may hold values from 32 to 256, as said below
- owner: int32 [16], replicated, may hold values from 0 to 7, as said below
Outputs:
- scored: bfloat16 [16, 256, 8192], P('group', None, 'prefix')
Inputs may be any that keep to these rules, and one draw needn't show every extreme that they name: Passage lengths; some passage has exactly 256 tokens in every draw. Every group number is the owner of exactly 2 passages.
All inputs are finite; a program needn't handle non-finite values.
Results may differ from a plain program's by a relative error of at most 0.0095.
Values may be sent and summed in bfloat16 or wider, within the bound.
No kernel may reach another device: no remote copies, remote signals or barrier semaphores. Data moves between devices by JAX's collectives and lax.ppermute only.
A program may use at most 192 MiB of HBM per device.

v0:
```python
import functools
import math

import jax
import jax.numpy as jnp
from jax import lax
from jax.experimental import pallas as pl
from jax.experimental.pallas import tpu as pltpu
from jax.sharding import PartitionSpec as P

H = 64
KVH = 8
HD = 128
NT = (((1,), (1,)), ((), ()))
NN = (((1,), (0,)), ((), ()))
SCALE = math.log2(math.e) / math.sqrt(HD)
LOW = -1e30
LIMIT = 60 * 2**20
HBM = pl.BlockSpec(memory_space=pltpu.HBM)
VMEM = pl.BlockSpec(memory_space=pltpu.VMEM)
SMEM = pl.BlockSpec(memory_space=pltpu.SMEM)
ANY = pl.BlockSpec(memory_space=pl.ANY)
TB = 32
RB = 16
KB = 256


def prep_kernel(info, kv, kvsend, slab, sem):
    rows = pl.ds(pl.multiple_of(info[3] * HD, HD), HD)
    copy = pltpu.make_async_copy(kv.at[rows, :], slab, sem)
    copy.start()
    copy.wait()
    for dest in range(16):
        for half in range(2):
            column = (half * KVH + dest // 2) * HD
            kvsend[dest, :, half * HD : (half + 1) * HD] = slab[:, column : column + HD]


def prep(info, kv):
    return pl.pallas_call(
        prep_kernel,
        out_shape=jax.ShapeDtypeStruct((16, 128, 256), jnp.bfloat16),
        in_specs=[SMEM, ANY],
        out_specs=VMEM,
        scratch_shapes=[pltpu.VMEM((HD, 2048), jnp.bfloat16), pltpu.SemaphoreType.DMA],
        compiler_params=pltpu.CompilerParams(vmem_limit_bytes=LIMIT),
        name="prep",
    )(info, kv)


def rank(owner, place, count):
    for o in range(8):
        count[o] = 0
    for i in range(16):
        o = owner[i]
        place[o * 2 + count[o]] = i
        count[o] = count[o] + 1


def blocks_of(length, core):
    return (length - TB * core + (2 * TB - 1)) >> 6


def packed_stats(tops, totals):
    lane = lax.broadcasted_iota(jnp.int32, (TB, HD), 1)
    kind = lane & 7
    first, second = (jnp.where(kind < 3, tops[h], totals[h]) for h in range(2))
    value = jnp.where((lane & 8) == 0, first, second)
    hi = value.astype(jnp.bfloat16).astype(jnp.float32)
    mid = (value - hi).astype(jnp.bfloat16).astype(jnp.float32)
    low = jnp.where((kind == 2) | (kind == 5), value - hi - mid, 0.0)
    value = jnp.where((kind == 0) | (kind == 3), hi, low)
    value = jnp.where((kind == 1) | (kind == 4), mid, value)
    return value


def load_queries(bufs, x, columns, qraw, sem):
    into = [qraw.at[(x + shift) & 3] for shift in (0, 3, 1)]
    into += [qraw.at[(x + 2) & 3, 0:8], qraw.at[(x + 2) & 3, 8:16]]
    copies = [
        pltpu.make_async_copy(b.at[:, :, columns], to, sem.at[i])
        for i, (b, to) in enumerate(zip(bufs, into))
    ]
    for c in copies:
        c.start()
    return copies


def flash_kernel(half, owner, lengths, info, *rest):
    bufs, rest = rest[:5], rest[5:]
    kv0, kv1 = rest[:2]
    outs, rest = rest[2:6], rest[6:]
    hold, held, qraw, qs, k1, v1, both, place, count, table, sem = rest
    x, core = info[1], info[2]
    copies = load_queries(bufs, x, slice(half * 256, half * 256 + 256), qraw, sem)
    loads = []
    for side, kv in enumerate((kv0, kv1)):
        for part in range(2):
            loads.append(
                pltpu.make_async_copy(
                    kv.at[part * 1024 : (part + 1) * 1024, :],
                    both.at[pl.ds(side * 2048 + part * 1024, 1024), :],
                    sem.at[5 + side * 2 + part],
                )
            )
            loads[-1].start()
    v1[:, HD : 2 * HD] = jnp.ones((4096, HD), jnp.bfloat16)
    rank(owner, place, count)
    total = 0
    for k in range(16):
        at = ((x + k // 4) & 3) * 4 + k % 4
        size = blocks_of(lengths[place[at]], core)

        @pl.loop(0, size)
        def _(t, k=k, total=total):
            table[total + t] = k * 4 + t

        total = total + size
    for spare in range(2 * RB):
        table[total + spare] = 0
    for c in copies:
        c.wait()

    def gather(first, count, into):
        for i in range(count):
            code = table[first + i]
            at = ((x + (code >> 4)) & 3) * 4 + ((code >> 2) & 3)
            for h in range(2):
                block = qraw[code & 3, place[at], :, h * HD : (h + 1) * HD]
                scaled = block.astype(jnp.float32) * SCALE
                high = scaled.astype(jnp.bfloat16)
                rows = slice((h * count + i) * TB, (h * count + i + 1) * TB)
                qs[into, rows, 0:HD] = high
                qs[into, rows, HD : 2 * HD] = (scaled - high.astype(jnp.float32)).astype(
                    jnp.bfloat16
                )

    gather(0, RB, 0)
    for part, c in enumerate(loads):
        c.wait()
        rows = slice(part * 1024, (part + 1) * 1024)
        k1[rows, 0:HD] = both[rows, 0:HD]
        k1[rows, HD : 2 * HD] = both[rows, 0:HD]
        v1[rows, 0:HD] = both[rows, HD : 2 * HD]
    lane = lax.broadcasted_iota(jnp.int32, (TB, HD), 1) >> 4

    def attend(q, first, count):
        top = jnp.full((2 * count * TB, HD), LOW, jnp.float32)
        acc = jnp.zeros((2 * count * TB, 2 * HD), jnp.float32)
        for j in range(4096 // KB):
            rows = slice(j * KB, (j + 1) * KB)
            s = lax.dot_general(q, k1[rows, :], NT, preferred_element_type=jnp.float32)
            new = jnp.maximum(top, jnp.max(s, axis=1, keepdims=True))
            p = jnp.exp2(s - new[:, 0:1]).astype(jnp.bfloat16)
            fade = jnp.exp2(top - new)
            acc = acc * jnp.concatenate([fade, fade], axis=1) + lax.dot_general(
                p, v1[rows, :], NN, preferred_element_type=jnp.float32
            )
            top = new
        for i in range(count):
            n = first + i
            code = table[n]
            d = jnp.where(n < total, code >> 4, 4)
            block = code & 15
            rows = pl.ds(pl.multiple_of(block * TB, TB), TB)
            tops, totals = [], []
            for h in range(2):
                r = (h * count + i) * TB
                hold[d, rows, h * HD : (h + 1) * HD] = acc[r : r + TB, 0:HD].astype(jnp.bfloat16)
                tops.append(top[r : r + TB, :])
                totals.append(acc[r : r + TB, HD : 2 * HD])
            group = block >> 3
            held[d, group] = jnp.where(
                lane == (block & 7), packed_stats(tops, totals), held[d, group]
            )

    rest_of = total & (RB - 1)
    few = (rest_of > 0) & (rest_of <= RB // 2)
    whole = (total >> 4) + (rest_of > RB // 2).astype(jnp.int32)

    @pl.loop(0, whole)
    def _(rb):
        q = qs[rb & 1]
        gather((rb + 1) * RB, RB, (rb + 1) & 1)
        attend(q, rb * RB, RB)

    @pl.when(few)
    def _():
        gather(whole * RB, RB // 2, 0)
        attend(qs[0, 0 : RB * TB], whole * RB, RB // 2)

    copies = []
    for d in range(4):
        for group in range(2):
            hold[d, 512:544, group * HD : (group + 1) * HD] = held[d, group].astype(jnp.bfloat16)
        copies.append(pltpu.make_async_copy(hold.at[d], outs[d], sem.at[d]))
        copies[-1].start()
    for c in copies:
        c.wait()


PART = jax.ShapeDtypeStruct((544, 256), jnp.bfloat16)


def flash(half, owner, lengths, info, bufs, kv0, kv1):
    return pl.pallas_call(
        functools.partial(flash_kernel, half),
        out_shape=(PART,) * 4,
        in_specs=[SMEM, SMEM, SMEM] + [ANY] * 7,
        out_specs=(ANY,) * 4,
        scratch_shapes=[
            pltpu.VMEM((5, 544, 256), jnp.bfloat16),
            pltpu.VMEM((5, 2, TB, HD), jnp.float32),
            pltpu.VMEM((4, 16, TB, 256), jnp.bfloat16),
            pltpu.VMEM((2, 2 * RB * TB, 2 * HD), jnp.bfloat16),
            pltpu.VMEM((4096, 2 * HD), jnp.bfloat16),
            pltpu.VMEM((4096, 2 * HD), jnp.bfloat16),
            pltpu.VMEM((4096, 2 * HD), jnp.bfloat16),
            pltpu.SMEM((16,), jnp.int32),
            pltpu.SMEM((8,), jnp.int32),
            pltpu.SMEM((64 + 2 * RB,), jnp.int32),
            pltpu.SemaphoreType.DMA((11,)),
        ],
        compiler_params=pltpu.CompilerParams(vmem_limit_bytes=LIMIT),
        cost_estimate=pl.CostEstimate(
            flops=2 * 2 * 4096 * 4096 * 256, bytes_accessed=5 * 2**20, transcendentals=2**24
        ),
        name="flash",
    )(owner, lengths, info, *bufs, kv0, kv1)


def own_kernel(owner, info, *rest):
    bufs, rest = rest[:5], rest[5:]
    okv, out0, out1, qraw, place, count, sem = rest
    x, core = info[1], info[2]
    rank(owner, place, count)
    copies = []
    for slot in range(4):
        i = place[x * 4 + slot]
        for b in range(4):
            into, done = qraw.at[(x + (0, 3, 1, 2)[b]) & 3, slot], sem.at[slot * 4 + b]
            if b < 3:
                copies.append(pltpu.make_async_copy(bufs[b].at[i], into, done))
                copies[-1].start()
            else:
                lower = pltpu.make_async_copy(bufs[3].at[i & 7], into, done)
                upper = pltpu.make_async_copy(bufs[4].at[i & 7], into, done)
                pl.when(i < 8)(lower.start)
                pl.when(i >= 8)(upper.start)
                copies.append(lower)
    held = [[jnp.zeros((TB, HD), jnp.float32) for _ in range(2)] for _ in range(2)]
    lane = lax.broadcasted_iota(jnp.int32, (TB, HD), 1) >> 4
    for c in copies:
        c.wait()
    row = lax.broadcasted_iota(jnp.int32, (512, 256), 0)
    token = ((row & 127) >> 5) * (2 * TB) + core * TB + (row & (TB - 1))
    allowed = lax.broadcasted_iota(jnp.int32, (512, 256), 1) <= token
    for slot in range(4):
        q = jnp.concatenate(
            [qraw[tb, slot, :, h * HD : (h + 1) * HD] for h in range(4) for tb in range(4)], axis=0
        )
        base = slot * 256
        keys = jnp.concatenate([okv[t, :, base : base + HD] for t in range(8)], axis=0)
        vals = jnp.concatenate([okv[t, :, base + HD : base + 256] for t in range(8)], axis=0)
        vals = jnp.concatenate([vals, jnp.ones((256, HD), jnp.bfloat16)], axis=1)
        s = lax.dot_general(q, keys, NT, preferred_element_type=jnp.float32) * SCALE
        top = jnp.max(jnp.where(allowed, s, -jnp.inf), axis=1, keepdims=True)
        p = jnp.where(allowed, jnp.exp2(jnp.minimum(s - top, 0.0)), 0.0).astype(jnp.bfloat16)
        acc = lax.dot_general(p, vals, NN, preferred_element_type=jnp.float32)
        top = jnp.broadcast_to(top, (512, HD))
        for half, out in enumerate((out0, out1)):
            for h in range(2):
                r = (half * 2 + h) * 128
                out[slot * 128 : (slot + 1) * 128, h * HD : (h + 1) * HD] = acc[
                    r : r + 128, 0:HD
                ].astype(jnp.bfloat16)
            for tb in range(4):
                block = slot * 4 + tb
                r = [(half * 2 + h) * 128 + tb * TB for h in range(2)]
                st = packed_stats(
                    [top[a : a + TB, :] for a in r], [acc[a : a + TB, HD : 2 * HD] for a in r]
                )
                held[half][block // 8] = jnp.where(lane == block % 8, st, held[half][block // 8])
    for half, out in enumerate((out0, out1)):
        for group in range(2):
            out[512:544, group * HD : (group + 1) * HD] = held[half][group].astype(jnp.bfloat16)


def own_part(owner, info, bufs, okv):
    return pl.pallas_call(
        own_kernel,
        out_shape=(PART,) * 2,
        in_specs=[SMEM, SMEM] + [HBM] * 5 + [VMEM],
        out_specs=(VMEM,) * 2,
        scratch_shapes=[
            pltpu.VMEM((4, 4, TB, 512), jnp.bfloat16),
            pltpu.SMEM((16,), jnp.int32),
            pltpu.SMEM((8,), jnp.int32),
            pltpu.SemaphoreType.DMA((16,)),
        ],
        compiler_params=pltpu.CompilerParams(vmem_limit_bytes=16 * 2**20),
        cost_estimate=pl.CostEstimate(
            flops=2 * 2 * 2048 * 256 * 256, bytes_accessed=4 * 2**20, transcendentals=2**19
        ),
        name="own_part",
    )(owner, info, *bufs, okv)


def combine_kernel(step, owner, lengths, info, *rest):
    parts, rest = rest[:5], rest[5:]
    if step > 0:
        first, rest = rest[0], rest[1:]
    if step == 2:
        got, rest = rest[0], rest[1:]
    out, body, tail, place, count, sem = rest
    x, core = info[1], info[2]
    group = (0, 1 - core, core)[step]
    size = 512 if step == 0 else 256
    rows = pl.ds(pl.multiple_of(group * 256, 256), size)
    columns = pl.ds(pl.multiple_of(group * HD, HD), size // 2)
    copies = []
    for i, part in enumerate(parts):
        copies.append(pltpu.make_async_copy(part.at[rows, :], body.at[i], sem.at[2 * i]))
        copies.append(
            pltpu.make_async_copy(part.at[512:544, columns], tail.at[i], sem.at[2 * i + 1])
        )
    for c in copies:
        c.start()
    rank(owner, place, count)
    lane = lax.broadcasted_iota(jnp.int32, (HD, 512), 0)
    col = lax.broadcasted_iota(jnp.int32, (HD, 512), 1)
    kind = (lane & 7) - 3 * (col >> 8)
    pick = (((lane >> 3) & 1) == ((col >> 7) & 1)) & (kind >= 0) & (kind < 3)
    pick = pick.astype(jnp.float32).astype(jnp.bfloat16)
    block = lax.broadcasted_iota(jnp.int32, (TB, HD), 1) >> 4
    row = lax.broadcasted_iota(jnp.int32, (128, 1), 0)
    token = (row >> 5) * (2 * TB) + core * TB + (row & (TB - 1))

    def target(slot, tb, of):
        return pl.ds(pl.multiple_of(slot * 256 + tb * 64 + of * TB, TB), TB)

    if step == 1:
        out[:, 0:256] = first[rows, :]
    if step == 2:
        for slot in range(2):
            for tb in range(4):
                place_of = pl.ds(pl.multiple_of(group * 256 + slot * 128 + tb * TB, TB), TB)
                out[target(slot, tb, core), 0:256] = first[place_of, :]
                out[target(slot, tb, 1 - core), :] = got[
                    slot * 128 + tb * TB : slot * 128 + (tb + 1) * TB, :
                ]
    for c in copies:
        c.wait()
    for slot in range(size // 128):
        valid = token < lengths[place[(x * 2 + group) * 2 + slot]]
        wide = []
        for i in range(5):
            st = tail[i, :, (slot // 2) * HD : (slot // 2 + 1) * HD].astype(jnp.float32)
            st = jnp.concatenate(
                [jnp.where(block == (slot % 2) * 4 + b, st, 0.0) for b in range(4)], axis=0
            )
            wide.append(
                lax.dot_general(
                    st.astype(jnp.bfloat16), pick, NN, preferred_element_type=jnp.float32
                )
            )
        top = functools.reduce(jnp.maximum, [w[:, 0:256] for w in wide])
        numer, denom = 0.0, 0.0
        for i, w in enumerate(wide):
            f = jnp.exp2(w[:, 0:256] - top)
            numer = numer + body[i, slot * 128 : (slot + 1) * 128, :].astype(jnp.float32) * f
            denom = denom + w[:, 256:512] * f
        done = jnp.where(valid, numer / denom, 0.0).astype(jnp.bfloat16)
        if step == 0:
            out[slot * 128 : (slot + 1) * 128, :] = done
        elif step == 1:
            out[slot * 128 : (slot + 1) * 128, 256:512] = done
        else:
            for tb in range(4):
                out[target(slot, tb, core), 256:512] = done[tb * TB : (tb + 1) * TB, :]


def combine(step, owner, lengths, info, parts, *more):
    size = 512 if step == 0 else 256
    shape = ((512, 256), (256, 512), (512, 512))[step]
    return pl.pallas_call(
        functools.partial(combine_kernel, step),
        out_shape=jax.ShapeDtypeStruct(shape, jnp.bfloat16),
        in_specs=[SMEM, SMEM, SMEM] + [ANY] * 5 + [VMEM] * step,
        out_specs=VMEM,
        scratch_shapes=[
            pltpu.VMEM((5, size, 256), jnp.bfloat16),
            pltpu.VMEM((5, TB, size // 2), jnp.bfloat16),
            pltpu.SMEM((16,), jnp.int32),
            pltpu.SMEM((8,), jnp.int32),
            pltpu.SemaphoreType.DMA((10,)),
        ],
        compiler_params=pltpu.CompilerParams(vmem_limit_bytes=12 * 2**20),
        name=f"combine_{step}",
    )(owner, lengths, info, *parts, *more)


def split_kernel(info, owner, left, right, cand, lower, upper, okvsend, own, count, sem):
    head = pl.multiple_of(info[0] * HD, HD)
    copies = [
        pltpu.make_async_copy(left.at[0:8], lower, sem.at[0]),
        pltpu.make_async_copy(right.at[8:16], upper, sem.at[1]),
        pltpu.make_async_copy(cand.at[:, :, pl.ds(head, HD)], own.at[:, :, 0:HD], sem.at[2]),
        pltpu.make_async_copy(
            cand.at[:, :, pl.ds(pl.multiple_of(head + KVH * HD, HD), HD)],
            own.at[:, :, HD : 2 * HD],
            sem.at[3],
        ),
    ]
    for c in copies:
        c.start()
    for o in range(8):
        count[o] = 0
    for c in copies:
        c.wait()
    for i in range(16):
        o = owner[i]
        slot = (o & 1) * 2 + count[o]
        count[o] = count[o] + 1
        for s in range(4):

            @pl.when(slot == s)
            def _(i=i, s=s, x=o >> 1):
                for core in range(2):
                    okvsend[x * 2 + core, :, s * 256 : (s + 1) * 256] = own[i]


def split(info, owner, left, right, cand):
    return pl.pallas_call(
        split_kernel,
        out_shape=(jax.ShapeDtypeStruct((8, 32, 512), jnp.bfloat16),) * 2
        + (jax.ShapeDtypeStruct((8, 32, 1024), jnp.bfloat16),),
        in_specs=[SMEM, SMEM, ANY, ANY, ANY],
        out_specs=(VMEM,) * 3,
        scratch_shapes=[
            pltpu.VMEM((16, 32, 256), jnp.bfloat16),
            pltpu.SMEM((8,), jnp.int32),
            pltpu.SemaphoreType.DMA((4,)),
        ],
        compiler_params=pltpu.CompilerParams(vmem_limit_bytes=LIMIT),
        cost_estimate=pl.CostEstimate(
            flops=2 * 10**11, bytes_accessed=2**21, transcendentals=0
        ),
        name="split",
    )(info, owner, left, right, cand)


CORE = [(i, i ^ 1) for i in range(8)]


def along_x(shift):
    return [(i, (i + 2 * shift) % 8) for i in range(8)]


def local(queries, cand_kv, prefix_kv, lengths, owner):
    g = lax.axis_index("group")
    info = jnp.stack([lax.axis_index("prefix") // 2, g // 2, g % 2, g]).astype(jnp.int32)
    swap = lambda a: lax.ppermute(a, "group", CORE)
    left = lax.ppermute(queries, "group", along_x(1))
    right = lax.ppermute(queries, "group", along_x(3))
    kvsend = prep(info, prefix_kv)
    kv0 = lax.all_to_all(kvsend, "prefix", split_axis=0, concat_axis=0, tiled=True)
    lower, upper, okvsend = split(info, owner, left, right, cand_kv)
    lower = lax.ppermute(lower, "group", along_x(1))
    upper = lax.ppermute(upper, "group", along_x(3))
    kv0, lower, upper = lax.optimization_barrier((kv0, lower, upper))
    kv0 = kv0.reshape(2048, 256)
    kv1 = swap(kv0)
    bufs = [queries, left, right, lower, upper]
    okvsend, _ = lax.optimization_barrier((okvsend, kv0))
    okv = lax.all_to_all(okvsend, "group", split_axis=0, concat_axis=0, tiled=True)
    send = lambda outs: [lax.ppermute(o, "group", along_x(s + 1)) for s, o in enumerate(outs)]
    mine0, *sent = flash(0, owner, lengths, info, bufs, kv0, kv1)
    got0 = send(sent)
    mine1, *sent = flash(1, owner, lengths, info, bufs, kv0, kv1)
    got1 = send(sent)
    okv, _ = lax.optimization_barrier((okv, mine1))
    own0, own1 = own_part(owner, info, bufs, okv)
    first = combine(0, owner, lengths, info, [mine0, *got0, own0])
    first, *got1 = lax.optimization_barrier((first, *got1))
    parts = [mine1, *got1, own1]
    got = swap(combine(1, owner, lengths, info, parts, first))
    return combine(2, owner, lengths, info, parts, first, got).reshape(2, 256, 512)


def solution(mesh):
    return jax.shard_map(
        local,
        mesh=mesh,
        in_specs=(P(None, "group", "prefix"), P(None, "group", None), P("prefix", None), P(), P()),
        out_specs=P("group", None, "prefix"),
        check_vma=False,
    )
```

profile of v0, /device:TPU:1, one launch (start us, length us, event | category | flops | bytes accessed | tf_op | source)
XLA Modules:
  0.0 103.4 jit_solution(1899427578187359730)
XLA Ops:
  0.0 3.3 %collective-permute-start.1 = (bf16[16,32,512]{2,1,0:T(8,128)(2,1)}, bf16[16,32,512]{2,1,0:T(8,128)(2,1)S(1)}, u32[]{:S(2)}, u32[]{:S(2)}) collective-permute-start(bf16[16,32,512]{2,1,0:T(8,128)(2,1)} %rest_0_.5), channel_id=1, source_target_pairs={{0,6},{1,7},{2,0},{3,1},{4,2},{5,3},{6,4},{7,5},{8,14},{9,15},{10,... | collective-permute-start | bytes 1572872 | tf_op jit(solution)/shard_map/ppermute | solution.py:465
  3.3 0.0 collective-permute-start
  3.3 0.7 pad_add_fusion.info
  4.0 2.8 %prep.1 = bf16[16,128,256]{2,1,0:T(8,128)(2,1)} custom-call(s32[4]{0:T(128)} %pad_add_fusion.info, bf16[1024,2048]{1,0:T(8,128)(2,1)} %kv.1), custom_call_target="tpu_custom_call" | custom-call | tf_op jit(solution)/shard_map/prep/pallas_call | solution.py:40
  6.8 7.8 %all-to-all-start = ((bf16[16,128,256]{2,1,0:T(8,128)(2,1)}), bf16[16,128,256]{2,1,0:T(8,128)(2,1)}, u32[]{:S(2)}, u32[]{:S(2)}) async-start(bf16[16,128,256]{2,1,0:T(8,128)(2,1)} %prep.1), calls=%async_computation | async-start | bytes 2097152 | tf_op jit(solution)/shard_map/all_to_all | solution.py:467
  14.6 0.0 collective-permute-done.1.right.rest_2_
  14.6 0.0 copy-start.2
  14.6 2.6 %collective-permute-done.left.rest_1_ = bf16[16,32,512]{2,1,0:T(8,128)(2,1)S(1)} collective-permute-done((bf16[16,32,512]{2,1,0:T(8,128)(2,1)}, bf16[16,32,512]{2,1,0:T(8,128)(2,1)S(1)}, u32[]{:S(2)}, u32[]{:S(2)}) %collective-permute-start) | collective-permute-done | bytes 524320 | tf_op jit(solution)/shard_map/ppermute | solution.py:464
  17.2 0.0 copy-done.2
  17.2 0.0 copy-start.4
  17.2 0.8 copy-done.4
  18.0 3.1 %split.1 = (bf16[8,32,512]{2,1,0:T(8,128)(2,1)}, bf16[8,32,512]{2,1,0:T(8,128)(2,1)}, bf16[8,32,1024]{2,1,0:T(8,128)(2,1)}) custom-call(s32[4]{0:T(128)} %pad_add_fusion.info, s32[16]{0:T(128)} %owner.13, bf16[16,32,512]{2,1,0:T(8,128)(2,1)} %copy-done.4, bf16[16,32,512]{2,1,0:T(8,128)(2,1)} %copy-done.2, bf16[16,32,2048]{2,1,0:T(8,128)(2,1)} %cand.1), custom_call_target="tpu_custom_call" | custom-call | flops 199999995904 | bytes 2097152 | tf_op jit(solution)/shard_map/split/pallas_call | solution.py:434
  21.1 0.1 collective-permute-start.2
  21.2 2.7 %collective-permute-start.3 = (bf16[8,32,512]{2,1,0:T(8,128)(2,1)}, bf16[8,32,512]{2,1,0:T(8,128)(2,1)S(1)}, u32[]{:S(2)}, u32[]{:S(2)}) collective-permute-start(bf16[8,32,512]{2,1,0:T(8,128)(2,1)} %get-tuple-element.28), channel_id=1, source_target_pairs={{0,6},{1,7},{2,0},{3,1},{4,2},{5,3},{6,4},{7,5},{8,14},{9,15},{10,... | collective-permute-start | bytes 786440 | tf_op jit(solution)/shard_map/ppermute | solution.py:470
  23.9 4.8 %collective-permute-done.2.rest_3_ = bf16[8,32,512]{2,1,0:T(8,128)(2,1)S(1)} collective-permute-done((bf16[8,32,512]{2,1,0:T(8,128)(2,1)}, bf16[8,32,512]{2,1,0:T(8,128)(2,1)S(1)}, u32[]{:S(2)}, u32[]{:S(2)}) %collective-permute-start.2) | collective-permute-done | bytes 262176 | tf_op jit(solution)/shard_map/ppermute | solution.py:469
  28.7 0.0 copy-start.9
  28.7 0.0 collective-permute-done.3.rest_4_
  28.7 1.7 %all-to-all-done = bf16[16,128,256]{2,1,0:T(8,128)(2,1)} async-done(((bf16[16,128,256]{2,1,0:T(8,128)(2,1)}), bf16[16,128,256]{2,1,0:T(8,128)(2,1)}, u32[]{:S(2)}, u32[]{:S(2)}) %all-to-all-start) | async-done | bytes 1048608 | tf_op jit(solution)/shard_map/all_to_all | solution.py:467
  30.4 2.9 %collective-permute-start.4 = (bf16[2048,256]{1,0:T(8,128)(2,1)}, bf16[2048,256]{1,0:T(8,128)(2,1)S(1)}, u32[]{:S(2)}, u32[]{:S(2)}) collective-permute-start(bf16[2048,256]{1,0:T(8,128)(2,1)} %bitcast.4.rest_5_), channel_id=1, source_target_pairs={{0,1},{1,0},{2,3},{3,2},{4,5},{5,4},{6,7},{7,6},{8,9},{9,8},{10,11... | collective-permute-start | bytes 3145736 | tf_op jit(solution)/shard_map/ppermute | solution.py:463
  33.2 4.2 %all-to-all-start.1 = ((bf16[8,32,1024]{2,1,0:T(8,128)(2,1)}), bf16[8,32,1024]{2,1,0:T(8,128)(2,1)S(1)}, u32[]{:S(2)}, u32[]{:S(2)}) async-start(bf16[8,32,1024]{2,1,0:T(8,128)(2,1)} %get-tuple-element.38), calls=%async_computation.1 | async-start | bytes 1048576 | tf_op jit(solution)/shard_map/all_to_all | solution.py:476
  37.4 0.0 collective-permute-done.4.rest_6_
  37.5 0.0 copy-done.9
  37.5 0.0 copy-done.11
  37.5 0.0 copy-start.16
  37.5 0.9 copy-done.16
  38.4 17.0 %flash.3 = (bf16[544,256]{1,0:T(8,128)(2,1)}, bf16[544,256]{1,0:T(8,128)(2,1)}, bf16[544,256]{1,0:T(8,128)(2,1)}, bf16[544,256]{1,0:T(8,128)(2,1)}) custom-call(s32[16]{0:T(128)} %owner.13, s32[16]{0:T(128)} %lengths.9, s32[4]{0:T(128)} %pad_add_fusion.info, bf16[16,32,512]{2,1,0:T(8,128)(2,1)} %rest_0_.5, bf16[16,32,512]{2,1,0:T(8,128)(2,1)} %copy-done.4, ...), custom_call_target="tpu_custom_call" | custom-call | flops 17179869184 | bytes 5242880 | tf_op jit(solution)/shard_map/flash/pallas_call | solution.py:206
  55.5 1.5 %collective-permute-start.5 = (bf16[544,256]{1,0:T(8,128)(2,1)}, bf16[544,256]{1,0:T(8,128)(2,1)S(1)}, u32[]{:S(2)}, u32[]{:S(2)}) collective-permute-start(bf16[544,256]{1,0:T(8,128)(2,1)} %get-tuple-element.34), channel_id=1, source_target_pairs={{0,2},{1,3},{2,4},{3,5},{4,6},{5,7},{6,0},{7,1},{8,10},{9,11},{10,... | collective-permute-start | bytes 835592 | tf_op jit(solution)/shard_map/ppermute | solution.py:477
  56.9 2.4 %collective-permute-start.6 = (bf16[544,256]{1,0:T(8,128)(2,1)}, bf16[544,256]{1,0:T(8,128)(2,1)}, u32[]{:S(2)}, u32[]{:S(2)}) collective-permute-start(bf16[544,256]{1,0:T(8,128)(2,1)} %get-tuple-element.35), channel_id=1, source_target_pairs={{0,4},{1,5},{2,6},{3,7},{4,0},{5,1},{6,2},{7,3},{8,12},{9,13},{10,... | collective-permute-start | bytes 835592 | tf_op jit(solution)/shard_map/ppermute | solution.py:477
  59.3 0.0 copy-start.14
  59.3 0.0 copy-start.6
  59.4 0.0 copy-start.15
  59.4 1.2 %collective-permute-start.7 = (bf16[544,256]{1,0:T(8,128)(2,1)}, bf16[544,256]{1,0:T(8,128)(2,1)}, u32[]{:S(2)}, u32[]{:S(2)}) collective-permute-start(bf16[544,256]{1,0:T(8,128)(2,1)} %get-tuple-element.36), channel_id=1, source_target_pairs={{0,6},{1,7},{2,0},{3,1},{4,2},{5,3},{6,4},{7,5},{8,14},{9,15},{10,... | collective-permute-start | bytes 835592 | tf_op jit(solution)/shard_map/ppermute | solution.py:477
  60.6 17.1 %flash.2 = (bf16[544,256]{1,0:T(8,128)(2,1)}, bf16[544,256]{1,0:T(8,128)(2,1)}, bf16[544,256]{1,0:T(8,128)(2,1)}, bf16[544,256]{1,0:T(8,128)(2,1)}) custom-call(s32[16]{0:T(128)} %owner.13, s32[16]{0:T(128)} %lengths.9, s32[4]{0:T(128)} %pad_add_fusion.info, bf16[16,32,512]{2,1,0:T(8,128)(2,1)} %rest_0_.5, bf16[16,32,512]{2,1,0:T(8,128)(2,1)} %copy-done.4, ...), custom_call_target="tpu_custom_call" | custom-call | flops 17179869184 | bytes 5242880 | tf_op jit(solution)/shard_map/flash/pallas_call | solution.py:206
  77.7 0.0 copy-start
  77.7 0.3 collective-permute-start.8
  78.0 1.1 %collective-permute-start.9 = (bf16[544,256]{1,0:T(8,128)(2,1)}, bf16[544,256]{1,0:T(8,128)(2,1)S(1)}, u32[]{:S(2)}, u32[]{:S(2)}) collective-permute-start(bf16[544,256]{1,0:T(8,128)(2,1)} %get-tuple-element.42), channel_id=1, source_target_pairs={{0,4},{1,5},{2,6},{3,7},{4,0},{5,1},{6,2},{7,3},{8,12},{9,13},{10,... | collective-permute-start | bytes 835592 | tf_op jit(solution)/shard_map/ppermute | solution.py:477
  79.1 0.0 collective-permute-done.5.rest_1_
  79.1 0.7 copy-done.7
  79.8 1.4 %collective-permute-start.10 = (bf16[544,256]{1,0:T(8,128)(2,1)}, bf16[544,256]{1,0:T(8,128)(2,1)S(1)}, u32[]{:S(2)}, u32[]{:S(2)}) collective-permute-start(bf16[544,256]{1,0:T(8,128)(2,1)} %get-tuple-element.43), channel_id=1, source_target_pairs={{0,6},{1,7},{2,0},{3,1},{4,2},{5,3},{6,4},{7,5},{8,14},{9,15},{10,... | collective-permute-start | bytes 835592 | tf_op jit(solution)/shard_map/ppermute | solution.py:477
  81.2 0.0 all-to-all-done.1.rest_5_
  81.2 0.0 copy-done.1
  81.3 0.0 copy-done.3
  81.3 0.0 copy-done.5
  81.3 0.0 copy-done.13
  81.3 0.0 copy-done.14
  81.3 0.0 copy-start.10
  81.3 0.9 copy-done.10
  82.2 0.9 copy-done.12
  83.2 2.8 %own_part.1 = (bf16[544,256]{1,0:T(8,128)(2,1)S(1)}, bf16[544,256]{1,0:T(8,128)(2,1)S(1)}) custom-call(s32[16]{0:T(128)S(1)} %copy-done.14, s32[4]{0:T(128)S(1)} %copy-done.13, bf16[16,32,512]{2,1,0:T(8,128)(2,1)S(1)} %copy-done.1, bf16[16,32,512]{2,1,0:T(8,128)(2,1)S(1)} %copy-done.5, bf16[16,32,512]{2,1,0:T(8,128)(2,1)S(1)} %copy-done.3, ...), custom_call_target="tpu_custom_call" | custom-call | flops 536870912 | bytes 4194304 | tf_op jit(solution)/shard_map/own_part/pallas_call | solution.py:290
  86.0 0.0 collective-permute-done.6.rest_2_
  86.0 0.0 collective-permute-done.7.rest_3_
  86.0 0.0 copy-done.6
  86.0 0.0 copy-done.15
  86.0 0.0 copy-start.8
  86.0 0.9 copy-done.8
  87.0 3.1 %combine_0.1.rest_5_ = bf16[512,256]{1,0:T(8,128)(2,1)S(1)} custom-call(s32[16]{0:T(128)S(1)} %copy-done.14, s32[16]{0:T(128)S(1)} %copy-done.15, s32[4]{0:T(128)S(1)} %copy-done.13, bf16[544,256]{1,0:T(8,128)(2,1)S(1)} %copy-done.6, bf16[544,256]{1,0:T(8,128)(2,1)S(1)} %copy-done.8, bf16[544,256]{1,0:T(8,128)(2,1)} %collective-permute-done.6.rest_2_, ...), custom_call_target="tpu_custom_call" | custom-call | tf_op jit(solution)/shard_map/combine_0/pallas_call | solution.py:386
  90.1 0.0 collective-permute-done.8.rest_1_
  90.1 0.0 collective-permute-done.9.rest_2_
  90.1 0.0 collective-permute-done.10.rest_3_
  90.1 0.0 copy-done
  90.1 2.4 %combine_1.1 = bf16[256,512]{1,0:T(8,128)(2,1)S(1)} custom-call(s32[16]{0:T(128)S(1)} %copy-done.14, s32[16]{0:T(128)S(1)} %copy-done.15, s32[4]{0:T(128)S(1)} %copy-done.13, bf16[544,256]{1,0:T(8,128)(2,1)S(1)} %copy-done, bf16[544,256]{1,0:T(8,128)(2,1)S(1)} %collective-permute-done.8.rest_1_, bf16[544,256]{1,0:T(8,128)(2,1)S(1)} %collective-permute-done.9.rest_2_, ...), custom_call_target="tpu_custom_call" | custom-call | tf_op jit(solution)/shard_map/combine_1/pallas_call | solution.py:386
  92.5 6.4 %collective-permute-start.11 = (bf16[256,512]{1,0:T(8,128)(2,1)S(1)}, bf16[256,512]{1,0:T(8,128)(2,1)S(1)}, u32[]{:S(2)}, u32[]{:S(2)}) collective-permute-start(bf16[256,512]{1,0:T(8,128)(2,1)S(1)} %combine_1.1), channel_id=1, source_target_pairs={{0,1},{1,0},{2,3},{3,2},{4,5},{5,4},{6,7},{7,6},{8,9},{9,8},{10,11... | collective-permute-start | bytes 786440 | tf_op jit(solution)/shard_map/ppermute | solution.py:463
  98.9 1.2 %collective-permute-done.11.rest_6_ = bf16[256,512]{1,0:T(8,128)(2,1)S(1)} collective-permute-done((bf16[256,512]{1,0:T(8,128)(2,1)S(1)}, bf16[256,512]{1,0:T(8,128)(2,1)S(1)}, u32[]{:S(2)}, u32[]{:S(2)}) %collective-permute-start.11) | collective-permute-done | bytes 262176 | tf_op jit(solution)/shard_map/ppermute | solution.py:463
  100.0 3.2 %combine_2.1 = bf16[512,512]{1,0:T(8,128)(2,1)} custom-call(s32[16]{0:T(128)S(1)} %copy-done.14, s32[16]{0:T(128)S(1)} %copy-done.15, s32[4]{0:T(128)S(1)} %copy-done.13, bf16[544,256]{1,0:T(8,128)(2,1)S(1)} %copy-done, bf16[544,256]{1,0:T(8,128)(2,1)S(1)} %collective-permute-done.8.rest_1_, bf16[544,256]{1,0:T(8,128)(2,1)S(1)} %collective-permute-done.9.rest_2_, ...), custom_call_target="tpu_custom_call" | custom-call | tf_op jit(solution)/shard_map/combine_2/pallas_call | solution.py:386
  (7 shorter events, 0.0 us)
Async XLA Ops:
  0.0 14.6 %collective-permute-start.1 = (bf16[16,32,512]{2,1,0:T(8,128)(2,1)}, bf16[16,32,512]{2,1,0:T(8,128)(2,1)S(1)}, u32[]{:S(2)}, u32[]{:S(2)}) collective-permute-start(bf16[16,32,512]{2,1,0:T(8,128)(2,1)} %rest_0_.5), channel_id=1, source_target_pairs={{0,6},{1,7},{2,0},{3,1},{4,2},{5,3},{6,4},{7,5},{8,14},{9,15},{10,... | collective-permute-start | bytes 1572872 | tf_op jit(solution)/shard_map/ppermute | solution.py:465
  3.3 13.9 %collective-permute-start = (bf16[16,32,512]{2,1,0:T(8,128)(2,1)}, bf16[16,32,512]{2,1,0:T(8,128)(2,1)S(1)}, u32[]{:S(2)}, u32[]{:S(2)}) collective-permute-start(bf16[16,32,512]{2,1,0:T(8,128)(2,1)} %rest_0_.5), channel_id=1, source_target_pairs={{0,2},{1,3},{2,4},{3,5},{4,6},{5,7},{6,0},{7,1},{8,10},{9,11},{10,... | collective-permute-start | bytes 1572872 | tf_op jit(solution)/shard_map/ppermute | solution.py:464
  6.8 23.6 %all-to-all-start = ((bf16[16,128,256]{2,1,0:T(8,128)(2,1)}), bf16[16,128,256]{2,1,0:T(8,128)(2,1)}, u32[]{:S(2)}, u32[]{:S(2)}) async-start(bf16[16,128,256]{2,1,0:T(8,128)(2,1)} %prep.1), calls=%async_computation | async-start | bytes 2097152 | tf_op jit(solution)/shard_map/all_to_all | solution.py:467
  14.6 2.6 %copy-start.2 = (bf16[16,32,512]{2,1,0:T(8,128)(2,1)}, bf16[16,32,512]{2,1,0:T(8,128)(2,1)S(1)}, u32[]{:S(2)}) copy-start(bf16[16,32,512]{2,1,0:T(8,128)(2,1)S(1)} %collective-permute-done.1.right.rest_2_) | copy-start | bytes 1572868
  17.2 0.8 copy-start.4
  21.1 7.5 %collective-permute-start.2 = (bf16[8,32,512]{2,1,0:T(8,128)(2,1)}, bf16[8,32,512]{2,1,0:T(8,128)(2,1)S(1)}, u32[]{:S(2)}, u32[]{:S(2)}) collective-permute-start(bf16[8,32,512]{2,1,0:T(8,128)(2,1)} %get-tuple-element.27), channel_id=1, source_target_pairs={{0,2},{1,3},{2,4},{3,5},{4,6},{5,7},{6,0},{7,1},{8,10},{9,11},{10,... | collective-permute-start | bytes 786440 | tf_op jit(solution)/shard_map/ppermute | solution.py:469
  21.2 7.5 %collective-permute-start.3 = (bf16[8,32,512]{2,1,0:T(8,128)(2,1)}, bf16[8,32,512]{2,1,0:T(8,128)(2,1)S(1)}, u32[]{:S(2)}, u32[]{:S(2)}) collective-permute-start(bf16[8,32,512]{2,1,0:T(8,128)(2,1)} %get-tuple-element.28), channel_id=1, source_target_pairs={{0,6},{1,7},{2,0},{3,1},{4,2},{5,3},{6,4},{7,5},{8,14},{9,15},{10,... | collective-permute-start | bytes 786440 | tf_op jit(solution)/shard_map/ppermute | solution.py:470
  28.7 8.8 %copy-start.9 = (bf16[8,32,512]{2,1,0:T(8,128)(2,1)}, bf16[8,32,512]{2,1,0:T(8,128)(2,1)S(1)}, u32[]{:S(2)}) copy-start(bf16[8,32,512]{2,1,0:T(8,128)(2,1)S(1)} %collective-permute-done.2.rest_3_) | copy-start | bytes 786436
  28.7 8.8 %copy-start.11 = (bf16[8,32,512]{2,1,0:T(8,128)(2,1)}, bf16[8,32,512]{2,1,0:T(8,128)(2,1)S(1)}, u32[]{:S(2)}) copy-start(bf16[8,32,512]{2,1,0:T(8,128)(2,1)S(1)} %collective-permute-done.3.rest_4_) | copy-start | bytes 786436
  30.4 7.1 %collective-permute-start.4 = (bf16[2048,256]{1,0:T(8,128)(2,1)}, bf16[2048,256]{1,0:T(8,128)(2,1)S(1)}, u32[]{:S(2)}, u32[]{:S(2)}) collective-permute-start(bf16[2048,256]{1,0:T(8,128)(2,1)} %bitcast.4.rest_5_), channel_id=1, source_target_pairs={{0,1},{1,0},{2,3},{3,2},{4,5},{5,4},{6,7},{7,6},{8,9},{9,8},{10,11... | collective-permute-start | bytes 3145736 | tf_op jit(solution)/shard_map/ppermute | solution.py:463
  33.2 48.0 %all-to-all-start.1 = ((bf16[8,32,1024]{2,1,0:T(8,128)(2,1)}), bf16[8,32,1024]{2,1,0:T(8,128)(2,1)S(1)}, u32[]{:S(2)}, u32[]{:S(2)}) async-start(bf16[8,32,1024]{2,1,0:T(8,128)(2,1)} %get-tuple-element.38), calls=%async_computation.1 | async-start | bytes 1048576 | tf_op jit(solution)/shard_map/all_to_all | solution.py:476
  37.5 1.0 copy-start.16
  55.5 23.6 %collective-permute-start.5 = (bf16[544,256]{1,0:T(8,128)(2,1)}, bf16[544,256]{1,0:T(8,128)(2,1)S(1)}, u32[]{:S(2)}, u32[]{:S(2)}) collective-permute-start(bf16[544,256]{1,0:T(8,128)(2,1)} %get-tuple-element.34), channel_id=1, source_target_pairs={{0,2},{1,3},{2,4},{3,5},{4,6},{5,7},{6,0},{7,1},{8,10},{9,11},{10,... | collective-permute-start | bytes 835592 | tf_op jit(solution)/shard_map/ppermute | solution.py:477
  56.9 29.1 %collective-permute-start.6 = (bf16[544,256]{1,0:T(8,128)(2,1)}, bf16[544,256]{1,0:T(8,128)(2,1)}, u32[]{:S(2)}, u32[]{:S(2)}) collective-permute-start(bf16[544,256]{1,0:T(8,128)(2,1)} %get-tuple-element.35), channel_id=1, source_target_pairs={{0,4},{1,5},{2,6},{3,7},{4,0},{5,1},{6,2},{7,3},{8,12},{9,13},{10,... | collective-permute-start | bytes 835592 | tf_op jit(solution)/shard_map/ppermute | solution.py:477
  59.3 21.9 %copy-start.1 = (bf16[16,32,512]{2,1,0:T(8,128)(2,1)S(1)}, bf16[16,32,512]{2,1,0:T(8,128)(2,1)}, u32[]{:S(2)}) copy-start(bf16[16,32,512]{2,1,0:T(8,128)(2,1)} %rest_0_.5) | copy-start | bytes 1572868
  59.3 21.9 %copy-start.3 = (bf16[16,32,512]{2,1,0:T(8,128)(2,1)S(1)}, bf16[16,32,512]{2,1,0:T(8,128)(2,1)}, u32[]{:S(2)}) copy-start(bf16[16,32,512]{2,1,0:T(8,128)(2,1)} %copy-done.2) | copy-start | bytes 1572868
  59.3 21.9 %copy-start.5 = (bf16[16,32,512]{2,1,0:T(8,128)(2,1)S(1)}, bf16[16,32,512]{2,1,0:T(8,128)(2,1)}, u32[]{:S(2)}) copy-start(bf16[16,32,512]{2,1,0:T(8,128)(2,1)} %copy-done.4) | copy-start | bytes 1572868
  59.3 21.9 %copy-start.13 = (s32[4]{0:T(128)S(1)}, s32[4]{0:T(128)}, u32[]{:S(2)}) copy-start(s32[4]{0:T(128)} %pad_add_fusion.info) | copy-start | bytes 52
  59.3 21.9 %copy-start.14 = (s32[16]{0:T(128)S(1)}, s32[16]{0:T(128)}, u32[]{:S(2)}) copy-start(s32[16]{0:T(128)} %owner.13) | copy-start | bytes 196
  59.3 26.7 %copy-start.6 = (bf16[544,256]{1,0:T(8,128)(2,1)S(1)}, bf16[544,256]{1,0:T(8,128)(2,1)}, u32[]{:S(2)}) copy-start(bf16[544,256]{1,0:T(8,128)(2,1)} %get-tuple-element.33.rest_0_) | copy-start | bytes 835588
  59.4 26.7 %copy-start.15 = (s32[16]{0:T(128)S(1)}, s32[16]{0:T(128)}, u32[]{:S(2)}) copy-start(s32[16]{0:T(128)} %lengths.9) | copy-start | bytes 196
  59.4 26.6 %collective-permute-start.7 = (bf16[544,256]{1,0:T(8,128)(2,1)}, bf16[544,256]{1,0:T(8,128)(2,1)}, u32[]{:S(2)}, u32[]{:S(2)}) collective-permute-start(bf16[544,256]{1,0:T(8,128)(2,1)} %get-tuple-element.36), channel_id=1, source_target_pairs={{0,6},{1,7},{2,0},{3,1},{4,2},{5,3},{6,4},{7,5},{8,14},{9,15},{10,... | collective-permute-start | bytes 835592 | tf_op jit(solution)/shard_map/ppermute | solution.py:477
  77.7 12.4 %copy-start = (bf16[544,256]{1,0:T(8,128)(2,1)S(1)}, bf16[544,256]{1,0:T(8,128)(2,1)}, u32[]{:S(2)}) copy-start(bf16[544,256]{1,0:T(8,128)(2,1)} %get-tuple-element.32.rest_0_) | copy-start | bytes 835588
  77.7 12.4 %collective-permute-start.8 = (bf16[544,256]{1,0:T(8,128)(2,1)}, bf16[544,256]{1,0:T(8,128)(2,1)S(1)}, u32[]{:S(2)}, u32[]{:S(2)}) collective-permute-start(bf16[544,256]{1,0:T(8,128)(2,1)} %get-tuple-element.41), channel_id=1, source_target_pairs={{0,2},{1,3},{2,4},{3,5},{4,6},{5,7},{6,0},{7,1},{8,10},{9,11},{10,... | collective-permute-start | bytes 835592 | tf_op jit(solution)/shard_map/ppermute | solution.py:477
  78.0 12.0 %collective-permute-start.9 = (bf16[544,256]{1,0:T(8,128)(2,1)}, bf16[544,256]{1,0:T(8,128)(2,1)S(1)}, u32[]{:S(2)}, u32[]{:S(2)}) collective-permute-start(bf16[544,256]{1,0:T(8,128)(2,1)} %get-tuple-element.42), channel_id=1, source_target_pairs={{0,4},{1,5},{2,6},{3,7},{4,0},{5,1},{6,2},{7,3},{8,12},{9,13},{10,... | collective-permute-start | bytes 835592 | tf_op jit(solution)/shard_map/ppermute | solution.py:477
  79.1 0.7 copy-start.7
  79.8 10.3 %collective-permute-start.10 = (bf16[544,256]{1,0:T(8,128)(2,1)}, bf16[544,256]{1,0:T(8,128)(2,1)S(1)}, u32[]{:S(2)}, u32[]{:S(2)}) collective-permute-start(bf16[544,256]{1,0:T(8,128)(2,1)} %get-tuple-element.43), channel_id=1, source_target_pairs={{0,6},{1,7},{2,0},{3,1},{4,2},{5,3},{6,4},{7,5},{8,14},{9,15},{10,... | collective-permute-start | bytes 835592 | tf_op jit(solution)/shard_map/ppermute | solution.py:477
  81.3 1.0 copy-start.10
  82.2 0.9 copy-start.12
  86.0 1.0 copy-start.8
  92.5 7.6 %collective-permute-start.11 = (bf16[256,512]{1,0:T(8,128)(2,1)S(1)}, bf16[256,512]{1,0:T(8,128)(2,1)S(1)}, u32[]{:S(2)}, u32[]{:S(2)}) collective-permute-start(bf16[256,512]{1,0:T(8,128)(2,1)S(1)} %combine_1.1), channel_id=1, source_target_pairs={{0,1},{1,0},{2,3},{3,2},{4,5},{5,4},{6,7},{7,6},{8,9},{9,8},{10,11... | collective-permute-start | bytes 786440 | tf_op jit(solution)/shard_map/ppermute | solution.py:463
where the time goes:
time: 104 us; the launch traced here: 103 us
  Pallas kernels  51.4 us (49%)
  starting transfers between devices  35.3 us (34%)
  waiting for transfers between devices  10.2 us (10%)
  local copies, waits for them, and re-layouts  5.34 us (5%)
    pallas_call x2, Pallas kernels, flash(): pl.pallas_call(functools.partial(flash_kernel, half), out_shape=(PART,) *...  34.1 us
    ppermute x2, starting transfers between devices, local(): swap = lambda a: lax.ppermute(a, 'group', CORE)  9.27 us
    pallas_call x3, Pallas kernels, combine(): pl.pallas_call(functools.partial(combine_kernel, step), out_shape=jax.Sha...  8.6 us
    ppermute x6, starting transfers between devices, local(): lax.ppermute(o, 'group', along_x(s + 1))  7.93 us
    all_to_all x1, starting transfers between devices, local(): lax.all_to_all(kvsend, 'prefix', split_axis=0, concat_axis=0, tiled=True)  7.83 us
    unnamed x34, local copies, waits for them, and re-layouts  5.34 us
    ppermute x1, waiting for transfers between devices, local(): lower = lax.ppermute(lower, 'group', along_x(1))  4.78 us
    all_to_all x1, starting transfers between devices, local(): lax.all_to_all(okvsend, 'group', split_axis=0, concat_axis=0, tiled=True)  4.2 us
  transfers between devices with their start and end apart: 14, of which 4 were waited for; matrix products, arithmetic and copies ran while one was open for 1% of the time, Pallas kernels for 44%

commit v1 on v0

--- a/solution.py
+++ b/solution.py
@@ -310,8 +310,6 @@
     parts, rest = rest[:5], rest[5:]
     if step > 0:
         first, rest = rest[0], rest[1:]
-    if step == 2:
-        got, rest = rest[0], rest[1:]
     out, body, tail, place, count, sem = rest
     x, core = info[1], info[2]
     group = (0, 1 - core, core)[step]
@@ -336,19 +334,8 @@
     row = lax.broadcasted_iota(jnp.int32, (128, 1), 0)
     token = (row >> 5) * (2 * TB) + core * TB + (row & (TB - 1))
 
-    def target(slot, tb, of):
-        return pl.ds(pl.multiple_of(slot * 256 + tb * 64 + of * TB, TB), TB)
-
-    if step == 1:
+    if step > 0:
         out[:, 0:256] = first[rows, :]
-    if step == 2:
-        for slot in range(2):
-            for tb in range(4):
-                place_of = pl.ds(pl.multiple_of(group * 256 + slot * 128 + tb * TB, TB), TB)
-                out[target(slot, tb, core), 0:256] = first[place_of, :]
-                out[target(slot, tb, 1 - core), :] = got[
-                    slot * 128 + tb * TB : slot * 128 + (tb + 1) * TB, :
-                ]
     for c in copies:
         c.wait()
     for slot in range(size // 128):
@@ -373,20 +360,17 @@
         done = jnp.where(valid, numer / denom, 0.0).astype(jnp.bfloat16)
         if step == 0:
             out[slot * 128 : (slot + 1) * 128, :] = done
-        elif step == 1:
+        else:
             out[slot * 128 : (slot + 1) * 128, 256:512] = done
-        else:
-            for tb in range(4):
-                out[target(slot, tb, core), 256:512] = done[tb * TB : (tb + 1) * TB, :]
 
 
 def combine(step, owner, lengths, info, parts, *more):
     size = 512 if step == 0 else 256
-    shape = ((512, 256), (256, 512), (512, 512))[step]
+    shape = (512, 256) if step == 0 else (256, 512)
     return pl.pallas_call(
         functools.partial(combine_kernel, step),
         out_shape=jax.ShapeDtypeStruct(shape, jnp.bfloat16),
-        in_specs=[SMEM, SMEM, SMEM] + [ANY] * 5 + [VMEM] * step,
+        in_specs=[SMEM, SMEM, SMEM] + [ANY] * 5 + [VMEM] * len(more),
         out_specs=VMEM,
         scratch_shapes=[
             pltpu.VMEM((5, size, 256), jnp.bfloat16),
@@ -398,6 +382,27 @@
         compiler_params=pltpu.CompilerParams(vmem_limit_bytes=12 * 2**20),
         name=f"combine_{step}",
     )(owner, lengths, info, *parts, *more)
+
+
+def weave_kernel(info, mine, got, out):
+    core = info[2]
+    for slot in range(2):
+        for tb in range(4):
+            rows = slice(slot * 128 + tb * TB, slot * 128 + (tb + 1) * TB)
+            for of, value in ((core, mine), (1 - core, got)):
+                to = pl.ds(pl.multiple_of(slot * 256 + tb * 64 + of * TB, TB), TB)
+                out[to, :] = value[rows, :]
+
+
+def weave(info, mine, got):
+    return pl.pallas_call(
+        weave_kernel,
+        out_shape=jax.ShapeDtypeStruct((512, 512), jnp.bfloat16),
+        in_specs=[SMEM, VMEM, VMEM],
+        out_specs=VMEM,
+        compiler_params=pltpu.CompilerParams(vmem_limit_bytes=12 * 2**20),
+        name="weave",
+    )(info, mine, got)
 
 
 def split_kernel(info, owner, left, right, cand, lower, upper, okvsend, own, count, sem):
@@ -485,7 +490,8 @@
     first, *got1 = lax.optimization_barrier((first, *got1))
     parts = [mine1, *got1, own1]
     got = swap(combine(1, owner, lengths, info, parts, first))
-    return combine(2, owner, lengths, info, parts, first, got).reshape(2, 256, 512)
+    mine = combine(2, owner, lengths, info, parts, first)
+    return weave(info, mine, got).reshape(2, 256, 512)
 
 
 def solution(mesh):

time: 104 us -> 103 us (level)
  waiting for transfers between devices: 10.2 us -> 9.07 us
    pallas_call x0 -> x1, Pallas kernels: none -> 1.38 us  [weave(): pl.pallas_call(weave_kernel, out_shape=jax.ShapeDtypeStruct((512, 512), j...]
    ppermute x2, waiting for transfers between devices: 1.16 us -> 0.01 us  [local(): swap = lambda a: lax.ppermute(a, 'group', CORE)]
  transfers between devices with their start and end apart: 14 -> 14, of which waited for: 4 -> 3; matrix products, arithmetic and copies ran while one was open for 1% -> 1% of each run, Pallas kernels for 44% -> 47%
where the time goes in v1:
time: 103 us
  Pallas kernels  52 us (50%)
  starting transfers between devices  35.3 us (34%)
  waiting for transfers between devices  9.07 us (9%)
  local copies, waits for them, and re-layouts  5.34 us (5%)
    pallas_call x2, Pallas kernels, flash(): pl.pallas_call(functools.partial(flash_kernel, half), out_shape=(PART,) *...  34.1 us
    ppermute x2, starting transfers between devices, local(): swap = lambda a: lax.ppermute(a, 'group', CORE)  9.29 us
    ppermute x6, starting transfers between devices, local(): lax.ppermute(o, 'group', along_x(s + 1))  7.94 us
    all_to_all x1, starting transfers between devices, local(): lax.all_to_all(kvsend, 'prefix', split_axis=0, concat_axis=0, tiled=True)  7.83 us
    pallas_call x3, Pallas kernels, combine(): pl.pallas_call(functools.partial(combine_kernel, step), out_shape=jax.Sha...  7.78 us
    unnamed x34, local copies, waits for them, and re-layouts  5.34 us
    ppermute x1, waiting for transfers between devices, local(): lower = lax.ppermute(lower, 'group', along_x(1))  4.78 us
    all_to_all x1, starting transfers between devices, local(): lax.all_to_all(okvsend, 'group', split_axis=0, concat_axis=0, tiled=True)  4.2 us
  transfers between devices with their start and end apart: 14, of which 3 were waited for; matrix products, arithmetic and copies ran while one was open for 1% of the time, Pallas kernels for 47%

profile of v1, /device:TPU:1, one launch (start us, length us, event | category | flops | bytes accessed | tf_op | source)
XLA Modules:
  0.0 102.6 jit_solution(3997246122152436837)
XLA Ops:
  0.0 3.3 %collective-permute-start.1 = (bf16[16,32,512]{2,1,0:T(8,128)(2,1)}, bf16[16,32,512]{2,1,0:T(8,128)(2,1)S(1)}, u32[]{:S(2)}, u32[]{:S(2)}) collective-permute-start(bf16[16,32,512]{2,1,0:T(8,128)(2,1)} %rest_0_.5), channel_id=1, source_target_pairs={{0,6},{1,7},{2,0},{3,1},{4,2},{5,3},{6,4},{7,5},{8,14},{9,15},{10,... | collective-permute-start | bytes 1572872 | tf_op jit(solution)/shard_map/ppermute | solution.py:470
  3.3 0.0 collective-permute-start
  3.3 0.7 pad_add_fusion.info
  4.0 2.8 %prep.1 = bf16[16,128,256]{2,1,0:T(8,128)(2,1)} custom-call(s32[4]{0:T(128)} %pad_add_fusion.info, bf16[1024,2048]{1,0:T(8,128)(2,1)} %kv.1), custom_call_target="tpu_custom_call" | custom-call | tf_op jit(solution)/shard_map/prep/pallas_call | solution.py:40
  6.8 7.8 %all-to-all-start = ((bf16[16,128,256]{2,1,0:T(8,128)(2,1)}), bf16[16,128,256]{2,1,0:T(8,128)(2,1)}, u32[]{:S(2)}, u32[]{:S(2)}) async-start(bf16[16,128,256]{2,1,0:T(8,128)(2,1)} %prep.1), calls=%async_computation | async-start | bytes 2097152 | tf_op jit(solution)/shard_map/all_to_all | solution.py:472
  14.6 0.0 collective-permute-done.1.right.rest_2_
  14.6 0.0 copy-start.2
  14.6 2.6 %collective-permute-done.left.rest_1_ = bf16[16,32,512]{2,1,0:T(8,128)(2,1)S(1)} collective-permute-done((bf16[16,32,512]{2,1,0:T(8,128)(2,1)}, bf16[16,32,512]{2,1,0:T(8,128)(2,1)S(1)}, u32[]{:S(2)}, u32[]{:S(2)}) %collective-permute-start) | collective-permute-done | bytes 524320 | tf_op jit(solution)/shard_map/ppermute | solution.py:469
  17.2 0.0 copy-done.2
  17.2 0.0 copy-start.4
  17.2 0.8 copy-done.4
  18.0 3.1 %split.1 = (bf16[8,32,512]{2,1,0:T(8,128)(2,1)}, bf16[8,32,512]{2,1,0:T(8,128)(2,1)}, bf16[8,32,1024]{2,1,0:T(8,128)(2,1)}) custom-call(s32[4]{0:T(128)} %pad_add_fusion.info, s32[16]{0:T(128)} %owner.13, bf16[16,32,512]{2,1,0:T(8,128)(2,1)} %copy-done.4, bf16[16,32,512]{2,1,0:T(8,128)(2,1)} %copy-done.2, bf16[16,32,2048]{2,1,0:T(8,128)(2,1)} %cand.1), custom_call_target="tpu_custom_call" | custom-call | flops 199999995904 | bytes 2097152 | tf_op jit(solution)/shard_map/split/pallas_call | solution.py:439
  21.1 0.1 collective-permute-start.2
  21.2 2.7 %collective-permute-start.3 = (bf16[8,32,512]{2,1,0:T(8,128)(2,1)}, bf16[8,32,512]{2,1,0:T(8,128)(2,1)S(1)}, u32[]{:S(2)}, u32[]{:S(2)}) collective-permute-start(bf16[8,32,512]{2,1,0:T(8,128)(2,1)} %get-tuple-element.28), channel_id=1, source_target_pairs={{0,6},{1,7},{2,0},{3,1},{4,2},{5,3},{6,4},{7,5},{8,14},{9,15},{10,... | collective-permute-start | bytes 786440 | tf_op jit(solution)/shard_map/ppermute | solution.py:475
  23.9 4.8 %collective-permute-done.2.rest_3_ = bf16[8,32,512]{2,1,0:T(8,128)(2,1)S(1)} collective-permute-done((bf16[8,32,512]{2,1,0:T(8,128)(2,1)}, bf16[8,32,512]{2,1,0:T(8,128)(2,1)S(1)}, u32[]{:S(2)}, u32[]{:S(2)}) %collective-permute-start.2) | collective-permute-done | bytes 262176 | tf_op jit(solution)/shard_map/ppermute | solution.py:474
  28.7 0.0 collective-permute-done.3.rest_4_
  28.7 1.7 %all-to-all-done = bf16[16,128,256]{2,1,0:T(8,128)(2,1)} async-done(((bf16[16,128,256]{2,1,0:T(8,128)(2,1)}), bf16[16,128,256]{2,1,0:T(8,128)(2,1)}, u32[]{:S(2)}, u32[]{:S(2)}) %all-to-all-start) | async-done | bytes 1048608 | tf_op jit(solution)/shard_map/all_to_all | solution.py:472
  30.4 2.9 %collective-permute-start.4 = (bf16[2048,256]{1,0:T(8,128)(2,1)}, bf16[2048,256]{1,0:T(8,128)(2,1)S(1)}, u32[]{:S(2)}, u32[]{:S(2)}) collective-permute-start(bf16[2048,256]{1,0:T(8,128)(2,1)} %bitcast.4.rest_5_), channel_id=1, source_target_pairs={{0,1},{1,0},{2,3},{3,2},{4,5},{5,4},{6,7},{7,6},{8,9},{9,8},{10,11... | collective-permute-start | bytes 3145736 | tf_op jit(solution)/shard_map/ppermute | solution.py:468
  33.2 4.2 %all-to-all-start.1 = ((bf16[8,32,1024]{2,1,0:T(8,128)(2,1)}), bf16[8,32,1024]{2,1,0:T(8,128)(2,1)S(1)}, u32[]{:S(2)}, u32[]{:S(2)}) async-start(bf16[8,32,1024]{2,1,0:T(8,128)(2,1)} %get-tuple-element.38), calls=%async_computation.1 | async-start | bytes 1048576 | tf_op jit(solution)/shard_map/all_to_all | solution.py:481
  37.4 0.0 collective-permute-done.4.rest_6_
  37.5 0.0 copy-done.9
  37.5 0.0 copy-done.11
  37.5 0.0 copy-start.16
  37.5 0.9 copy-done.16
  38.4 17.0 %flash.3 = (bf16[544,256]{1,0:T(8,128)(2,1)}, bf16[544,256]{1,0:T(8,128)(2,1)}, bf16[544,256]{1,0:T(8,128)(2,1)}, bf16[544,256]{1,0:T(8,128)(2,1)}) custom-call(s32[16]{0:T(128)} %owner.13, s32[16]{0:T(128)} %lengths.9, s32[4]{0:T(128)} %pad_add_fusion.info, bf16[16,32,512]{2,1,0:T(8,128)(2,1)} %rest_0_.5, bf16[16,32,512]{2,1,0:T(8,128)(2,1)} %copy-done.4, ...), custom_call_target="tpu_custom_call" | custom-call | flops 17179869184 | bytes 5242880 | tf_op jit(solution)/shard_map/flash/pallas_call | solution.py:206
  55.5 1.5 %collective-permute-start.5 = (bf16[544,256]{1,0:T(8,128)(2,1)}, bf16[544,256]{1,0:T(8,128)(2,1)S(1)}, u32[]{:S(2)}, u32[]{:S(2)}) collective-permute-start(bf16[544,256]{1,0:T(8,128)(2,1)} %get-tuple-element.34), channel_id=1, source_target_pairs={{0,2},{1,3},{2,4},{3,5},{4,6},{5,7},{6,0},{7,1},{8,10},{9,11},{10,... | collective-permute-start | bytes 835592 | tf_op jit(solution)/shard_map/ppermute | solution.py:482
  56.9 2.4 %collective-permute-start.6 = (bf16[544,256]{1,0:T(8,128)(2,1)}, bf16[544,256]{1,0:T(8,128)(2,1)}, u32[]{:S(2)}, u32[]{:S(2)}) collective-permute-start(bf16[544,256]{1,0:T(8,128)(2,1)} %get-tuple-element.35), channel_id=1, source_target_pairs={{0,4},{1,5},{2,6},{3,7},{4,0},{5,1},{6,2},{7,3},{8,12},{9,13},{10,... | collective-permute-start | bytes 835592 | tf_op jit(solution)/shard_map/ppermute | solution.py:482
  59.3 0.0 copy-start.14
  59.3 0.0 copy-start.6
  59.4 0.0 copy-start.15
  59.4 1.3 %collective-permute-start.7 = (bf16[544,256]{1,0:T(8,128)(2,1)}, bf16[544,256]{1,0:T(8,128)(2,1)}, u32[]{:S(2)}, u32[]{:S(2)}) collective-permute-start(bf16[544,256]{1,0:T(8,128)(2,1)} %get-tuple-element.36), channel_id=1, source_target_pairs={{0,6},{1,7},{2,0},{3,1},{4,2},{5,3},{6,4},{7,5},{8,14},{9,15},{10,... | collective-permute-start | bytes 835592 | tf_op jit(solution)/shard_map/ppermute | solution.py:482
  60.6 17.1 %flash.2 = (bf16[544,256]{1,0:T(8,128)(2,1)}, bf16[544,256]{1,0:T(8,128)(2,1)}, bf16[544,256]{1,0:T(8,128)(2,1)}, bf16[544,256]{1,0:T(8,128)(2,1)}) custom-call(s32[16]{0:T(128)} %owner.13, s32[16]{0:T(128)} %lengths.9, s32[4]{0:T(128)} %pad_add_fusion.info, bf16[16,32,512]{2,1,0:T(8,128)(2,1)} %rest_0_.5, bf16[16,32,512]{2,1,0:T(8,128)(2,1)} %copy-done.4, ...), custom_call_target="tpu_custom_call" | custom-call | flops 17179869184 | bytes 5242880 | tf_op jit(solution)/shard_map/flash/pallas_call | solution.py:206
  77.7 0.0 copy-start
  77.7 0.4 collective-permute-start.8
  78.1 1.1 %collective-permute-start.9 = (bf16[544,256]{1,0:T(8,128)(2,1)}, bf16[544,256]{1,0:T(8,128)(2,1)S(1)}, u32[]{:S(2)}, u32[]{:S(2)}) collective-permute-start(bf16[544,256]{1,0:T(8,128)(2,1)} %get-tuple-element.42), channel_id=1, source_target_pairs={{0,4},{1,5},{2,6},{3,7},{4,0},{5,1},{6,2},{7,3},{8,12},{9,13},{10,... | collective-permute-start | bytes 835592 | tf_op jit(solution)/shard_map/ppermute | solution.py:482
  79.1 0.0 collective-permute-done.5.rest_1_
  79.1 0.7 copy-done.7
  79.8 1.4 %collective-permute-start.10 = (bf16[544,256]{1,0:T(8,128)(2,1)}, bf16[544,256]{1,0:T(8,128)(2,1)S(1)}, u32[]{:S(2)}, u32[]{:S(2)}) collective-permute-start(bf16[544,256]{1,0:T(8,128)(2,1)} %get-tuple-element.43), channel_id=1, source_target_pairs={{0,6},{1,7},{2,0},{3,1},{4,2},{5,3},{6,4},{7,5},{8,14},{9,15},{10,... | collective-permute-start | bytes 835592 | tf_op jit(solution)/shard_map/ppermute | solution.py:482
  81.3 0.0 all-to-all-done.1.rest_5_
  81.3 0.0 copy-done.1
  81.3 0.0 copy-done.3
  81.3 0.0 copy-done.5
  81.3 0.0 copy-done.13
  81.3 0.0 copy-done.14
  81.3 0.0 copy-start.10
  81.3 0.9 copy-done.10
  82.2 0.9 copy-done.12
  83.2 2.8 %own_part.1 = (bf16[544,256]{1,0:T(8,128)(2,1)S(1)}, bf16[544,256]{1,0:T(8,128)(2,1)S(1)}) custom-call(s32[16]{0:T(128)S(1)} %copy-done.14, s32[4]{0:T(128)S(1)} %copy-done.13, bf16[16,32,512]{2,1,0:T(8,128)(2,1)S(1)} %copy-done.1, bf16[16,32,512]{2,1,0:T(8,128)(2,1)S(1)} %copy-done.5, bf16[16,32,512]{2,1,0:T(8,128)(2,1)S(1)} %copy-done.3, ...), custom_call_target="tpu_custom_call" | custom-call | flops 536870912 | bytes 4194304 | tf_op jit(solution)/shard_map/own_part/pallas_call | solution.py:290
  86.0 0.0 collective-permute-done.6.rest_2_
  86.0 0.0 collective-permute-done.7.rest_3_
  86.0 0.0 copy-done.6
  86.0 0.0 copy-done.15
  86.0 0.0 copy-start.8
  86.0 0.9 copy-done.8
  87.0 3.1 %combine_0.1.rest_5_ = bf16[512,256]{1,0:T(8,128)(2,1)S(1)} custom-call(s32[16]{0:T(128)S(1)} %copy-done.14, s32[16]{0:T(128)S(1)} %copy-done.15, s32[4]{0:T(128)S(1)} %copy-done.13, bf16[544,256]{1,0:T(8,128)(2,1)S(1)} %copy-done.6, bf16[544,256]{1,0:T(8,128)(2,1)S(1)} %copy-done.8, bf16[544,256]{1,0:T(8,128)(2,1)} %collective-permute-done.6.rest_2_, ...), custom_call_target="tpu_custom_call" | custom-call | tf_op jit(solution)/shard_map/combine_0/pallas_call | solution.py:370
  90.1 0.0 collective-permute-done.8.rest_1_
  90.1 0.0 collective-permute-done.9.rest_2_
  90.1 0.0 collective-permute-done.10.rest_3_
  90.1 0.0 copy-done
  90.1 2.4 %combine_1.1 = bf16[256,512]{1,0:T(8,128)(2,1)S(1)} custom-call(s32[16]{0:T(128)S(1)} %copy-done.14, s32[16]{0:T(128)S(1)} %copy-done.15, s32[4]{0:T(128)S(1)} %copy-done.13, bf16[544,256]{1,0:T(8,128)(2,1)S(1)} %copy-done, bf16[544,256]{1,0:T(8,128)(2,1)S(1)} %collective-permute-done.8.rest_1_, bf16[544,256]{1,0:T(8,128)(2,1)S(1)} %collective-permute-done.9.rest_2_, ...), custom_call_target="tpu_custom_call" | custom-call | tf_op jit(solution)/shard_map/combine_1/pallas_call | solution.py:370
  92.5 6.4 %collective-permute-start.11 = (bf16[256,512]{1,0:T(8,128)(2,1)S(1)}, bf16[256,512]{1,0:T(8,128)(2,1)S(1)}, u32[]{:S(2)}, u32[]{:S(2)}) collective-permute-start(bf16[256,512]{1,0:T(8,128)(2,1)S(1)} %combine_1.1), channel_id=1, source_target_pairs={{0,1},{1,0},{2,3},{3,2},{4,5},{5,4},{6,7},{7,6},{8,9},{9,8},{10,11... | collective-permute-start | bytes 786440 | tf_op jit(solution)/shard_map/ppermute | solution.py:468
  98.9 2.3 %combine_2.1.mine = bf16[256,512]{1,0:T(8,128)(2,1)S(1)} custom-call(s32[16]{0:T(128)S(1)} %copy-done.14, s32[16]{0:T(128)S(1)} %copy-done.15, s32[4]{0:T(128)S(1)} %copy-done.13, bf16[544,256]{1,0:T(8,128)(2,1)S(1)} %copy-done, bf16[544,256]{1,0:T(8,128)(2,1)S(1)} %collective-permute-done.8.rest_1_, bf16[544,256]{1,0:T(8,128)(2,1)S(1)} %collective-permute-done.9.rest_2_, ...), custom_call_target="tpu_custom_call" | custom-call | tf_op jit(solution)/shard_map/combine_2/pallas_call | solution.py:370
  101.3 0.0 collective-permute-done.11.got
  101.3 1.4 %weave.1 = bf16[512,512]{1,0:T(8,128)(2,1)} custom-call(s32[4]{0:T(128)S(1)} %copy-done.13, bf16[256,512]{1,0:T(8,128)(2,1)S(1)} %combine_2.1.mine, bf16[256,512]{1,0:T(8,128)(2,1)S(1)} %collective-permute-done.11.got), custom_call_target="tpu_custom_call" | custom-call | tf_op jit(solution)/shard_map/weave/pallas_call | solution.py:398
  (8 shorter events, 0.0 us)
Async XLA Ops:
  0.0 14.6 %collective-permute-start.1 = (bf16[16,32,512]{2,1,0:T(8,128)(2,1)}, bf16[16,32,512]{2,1,0:T(8,128)(2,1)S(1)}, u32[]{:S(2)}, u32[]{:S(2)}) collective-permute-start(bf16[16,32,512]{2,1,0:T(8,128)(2,1)} %rest_0_.5), channel_id=1, source_target_pairs={{0,6},{1,7},{2,0},{3,1},{4,2},{5,3},{6,4},{7,5},{8,14},{9,15},{10,... | collective-permute-start | bytes 1572872 | tf_op jit(solution)/shard_map/ppermute | solution.py:470
  3.3 13.9 %collective-permute-start = (bf16[16,32,512]{2,1,0:T(8,128)(2,1)}, bf16[16,32,512]{2,1,0:T(8,128)(2,1)S(1)}, u32[]{:S(2)}, u32[]{:S(2)}) collective-permute-start(bf16[16,32,512]{2,1,0:T(8,128)(2,1)} %rest_0_.5), channel_id=1, source_target_pairs={{0,2},{1,3},{2,4},{3,5},{4,6},{5,7},{6,0},{7,1},{8,10},{9,11},{10,... | collective-permute-start | bytes 1572872 | tf_op jit(solution)/shard_map/ppermute | solution.py:469
  6.8 23.6 %all-to-all-start = ((bf16[16,128,256]{2,1,0:T(8,128)(2,1)}), bf16[16,128,256]{2,1,0:T(8,128)(2,1)}, u32[]{:S(2)}, u32[]{:S(2)}) async-start(bf16[16,128,256]{2,1,0:T(8,128)(2,1)} %prep.1), calls=%async_computation | async-start | bytes 2097152 | tf_op jit(solution)/shard_map/all_to_all | solution.py:472
  14.6 2.6 %copy-start.2 = (bf16[16,32,512]{2,1,0:T(8,128)(2,1)}, bf16[16,32,512]{2,1,0:T(8,128)(2,1)S(1)}, u32[]{:S(2)}) copy-start(bf16[16,32,512]{2,1,0:T(8,128)(2,1)S(1)} %collective-permute-done.1.right.rest_2_) | copy-start | bytes 1572868
  17.2 0.8 copy-start.4
  21.1 7.5 %collective-permute-start.2 = (bf16[8,32,512]{2,1,0:T(8,128)(2,1)}, bf16[8,32,512]{2,1,0:T(8,128)(2,1)S(1)}, u32[]{:S(2)}, u32[]{:S(2)}) collective-permute-start(bf16[8,32,512]{2,1,0:T(8,128)(2,1)} %get-tuple-element.27), channel_id=1, source_target_pairs={{0,2},{1,3},{2,4},{3,5},{4,6},{5,7},{6,0},{7,1},{8,10},{9,11},{10,... | collective-permute-start | bytes 786440 | tf_op jit(solution)/shard_map/ppermute | solution.py:474
  21.2 7.5 %collective-permute-start.3 = (bf16[8,32,512]{2,1,0:T(8,128)(2,1)}, bf16[8,32,512]{2,1,0:T(8,128)(2,1)S(1)}, u32[]{:S(2)}, u32[]{:S(2)}) collective-permute-start(bf16[8,32,512]{2,1,0:T(8,128)(2,1)} %get-tuple-element.28), channel_id=1, source_target_pairs={{0,6},{1,7},{2,0},{3,1},{4,2},{5,3},{6,4},{7,5},{8,14},{9,15},{10,... | collective-permute-start | bytes 786440 | tf_op jit(solution)/shard_map/ppermute | solution.py:475
  28.7 8.8 %copy-start.9 = (bf16[8,32,512]{2,1,0:T(8,128)(2,1)}, bf16[8,32,512]{2,1,0:T(8,128)(2,1)S(1)}, u32[]{:S(2)}) copy-start(bf16[8,32,512]{2,1,0:T(8,128)(2,1)S(1)} %collective-permute-done.2.rest_3_) | copy-start | bytes 786436
  28.7 8.8 %copy-start.11 = (bf16[8,32,512]{2,1,0:T(8,128)(2,1)}, bf16[8,32,512]{2,1,0:T(8,128)(2,1)S(1)}, u32[]{:S(2)}) copy-start(bf16[8,32,512]{2,1,0:T(8,128)(2,1)S(1)} %collective-permute-done.3.rest_4_) | copy-start | bytes 786436
  30.4 7.1 %collective-permute-start.4 = (bf16[2048,256]{1,0:T(8,128)(2,1)}, bf16[2048,256]{1,0:T(8,128)(2,1)S(1)}, u32[]{:S(2)}, u32[]{:S(2)}) collective-permute-start(bf16[2048,256]{1,0:T(8,128)(2,1)} %bitcast.4.rest_5_), channel_id=1, source_target_pairs={{0,1},{1,0},{2,3},{3,2},{4,5},{5,4},{6,7},{7,6},{8,9},{9,8},{10,11... | collective-permute-start | bytes 3145736 | tf_op jit(solution)/shard_map/ppermute | solution.py:468
  33.2 48.0 %all-to-all-start.1 = ((bf16[8,32,1024]{2,1,0:T(8,128)(2,1)}), bf16[8,32,1024]{2,1,0:T(8,128)(2,1)S(1)}, u32[]{:S(2)}, u32[]{:S(2)}) async-start(bf16[8,32,1024]{2,1,0:T(8,128)(2,1)} %get-tuple-element.38), calls=%async_computation.1 | async-start | bytes 1048576 | tf_op jit(solution)/shard_map/all_to_all | solution.py:481
  37.5 1.0 copy-start.16
  55.5 23.6 %collective-permute-start.5 = (bf16[544,256]{1,0:T(8,128)(2,1)}, bf16[544,256]{1,0:T(8,128)(2,1)S(1)}, u32[]{:S(2)}, u32[]{:S(2)}) collective-permute-start(bf16[544,256]{1,0:T(8,128)(2,1)} %get-tuple-element.34), channel_id=1, source_target_pairs={{0,2},{1,3},{2,4},{3,5},{4,6},{5,7},{6,0},{7,1},{8,10},{9,11},{10,... | collective-permute-start | bytes 835592 | tf_op jit(solution)/shard_map/ppermute | solution.py:482
  56.9 29.1 %collective-permute-start.6 = (bf16[544,256]{1,0:T(8,128)(2,1)}, bf16[544,256]{1,0:T(8,128)(2,1)}, u32[]{:S(2)}, u32[]{:S(2)}) collective-permute-start(bf16[544,256]{1,0:T(8,128)(2,1)} %get-tuple-element.35), channel_id=1, source_target_pairs={{0,4},{1,5},{2,6},{3,7},{4,0},{5,1},{6,2},{7,3},{8,12},{9,13},{10,... | collective-permute-start | bytes 835592 | tf_op jit(solution)/shard_map/ppermute | solution.py:482
  59.3 21.9 %copy-start.1 = (bf16[16,32,512]{2,1,0:T(8,128)(2,1)S(1)}, bf16[16,32,512]{2,1,0:T(8,128)(2,1)}, u32[]{:S(2)}) copy-start(bf16[16,32,512]{2,1,0:T(8,128)(2,1)} %rest_0_.5) | copy-start | bytes 1572868
  59.3 21.9 %copy-start.3 = (bf16[16,32,512]{2,1,0:T(8,128)(2,1)S(1)}, bf16[16,32,512]{2,1,0:T(8,128)(2,1)}, u32[]{:S(2)}) copy-start(bf16[16,32,512]{2,1,0:T(8,128)(2,1)} %copy-done.2) | copy-start | bytes 1572868
  59.3 21.9 %copy-start.5 = (bf16[16,32,512]{2,1,0:T(8,128)(2,1)S(1)}, bf16[16,32,512]{2,1,0:T(8,128)(2,1)}, u32[]{:S(2)}) copy-start(bf16[16,32,512]{2,1,0:T(8,128)(2,1)} %copy-done.4) | copy-start | bytes 1572868
  59.3 21.9 %copy-start.13 = (s32[4]{0:T(128)S(1)}, s32[4]{0:T(128)}, u32[]{:S(2)}) copy-start(s32[4]{0:T(128)} %pad_add_fusion.info) | copy-start | bytes 52
  59.3 22.0 %copy-start.14 = (s32[16]{0:T(128)S(1)}, s32[16]{0:T(128)}, u32[]{:S(2)}) copy-start(s32[16]{0:T(128)} %owner.13) | copy-start | bytes 196
  59.3 26.7 %copy-start.6 = (bf16[544,256]{1,0:T(8,128)(2,1)S(1)}, bf16[544,256]{1,0:T(8,128)(2,1)}, u32[]{:S(2)}) copy-start(bf16[544,256]{1,0:T(8,128)(2,1)} %get-tuple-element.33.rest_0_) | copy-start | bytes 835588
  59.4 26.7 %copy-start.15 = (s32[16]{0:T(128)S(1)}, s32[16]{0:T(128)}, u32[]{:S(2)}) copy-start(s32[16]{0:T(128)} %lengths.9) | copy-start | bytes 196
  59.4 26.6 %collective-permute-start.7 = (bf16[544,256]{1,0:T(8,128)(2,1)}, bf16[544,256]{1,0:T(8,128)(2,1)}, u32[]{:S(2)}, u32[]{:S(2)}) collective-permute-start(bf16[544,256]{1,0:T(8,128)(2,1)} %get-tuple-element.36), channel_id=1, source_target_pairs={{0,6},{1,7},{2,0},{3,1},{4,2},{5,3},{6,4},{7,5},{8,14},{9,15},{10,... | collective-permute-start | bytes 835592 | tf_op jit(solution)/shard_map/ppermute | solution.py:482
  77.7 12.4 %copy-start = (bf16[544,256]{1,0:T(8,128)(2,1)S(1)}, bf16[544,256]{1,0:T(8,128)(2,1)}, u32[]{:S(2)}) copy-start(bf16[544,256]{1,0:T(8,128)(2,1)} %get-tuple-element.32.rest_0_) | copy-start | bytes 835588
  77.7 12.4 %collective-permute-start.8 = (bf16[544,256]{1,0:T(8,128)(2,1)}, bf16[544,256]{1,0:T(8,128)(2,1)S(1)}, u32[]{:S(2)}, u32[]{:S(2)}) collective-permute-start(bf16[544,256]{1,0:T(8,128)(2,1)} %get-tuple-element.41), channel_id=1, source_target_pairs={{0,2},{1,3},{2,4},{3,5},{4,6},{5,7},{6,0},{7,1},{8,10},{9,11},{10,... | collective-permute-start | bytes 835592 | tf_op jit(solution)/shard_map/ppermute | solution.py:482
  78.1 12.0 %collective-permute-start.9 = (bf16[544,256]{1,0:T(8,128)(2,1)}, bf16[544,256]{1,0:T(8,128)(2,1)S(1)}, u32[]{:S(2)}, u32[]{:S(2)}) collective-permute-start(bf16[544,256]{1,0:T(8,128)(2,1)} %get-tuple-element.42), channel_id=1, source_target_pairs={{0,4},{1,5},{2,6},{3,7},{4,0},{5,1},{6,2},{7,3},{8,12},{9,13},{10,... | collective-permute-start | bytes 835592 | tf_op jit(solution)/shard_map/ppermute | solution.py:482
  79.1 0.7 copy-start.7
  79.8 10.3 %collective-permute-start.10 = (bf16[544,256]{1,0:T(8,128)(2,1)}, bf16[544,256]{1,0:T(8,128)(2,1)S(1)}, u32[]{:S(2)}, u32[]{:S(2)}) collective-permute-start(bf16[544,256]{1,0:T(8,128)(2,1)} %get-tuple-element.43), channel_id=1, source_target_pairs={{0,6},{1,7},{2,0},{3,1},{4,2},{5,3},{6,4},{7,5},{8,14},{9,15},{10,... | collective-permute-start | bytes 835592 | tf_op jit(solution)/shard_map/ppermute | solution.py:482
  81.3 1.0 copy-start.10
  82.2 0.9 copy-start.12
  86.0 1.0 copy-start.8
  92.5 8.8 %collective-permute-start.11 = (bf16[256,512]{1,0:T(8,128)(2,1)S(1)}, bf16[256,512]{1,0:T(8,128)(2,1)S(1)}, u32[]{:S(2)}, u32[]{:S(2)}) collective-permute-start(bf16[256,512]{1,0:T(8,128)(2,1)S(1)} %combine_1.1), channel_id=1, source_target_pairs={{0,1},{1,0},{2,3},{3,2},{4,5},{5,4},{6,7},{7,6},{8,9},{9,8},{10,11... | collective-permute-start | bytes 786440 | tf_op jit(solution)/shard_map/ppermute | solution.py:468
